TPU v7x, 256 devices: a whole 4x4x8 slice. The times are simulated.
256 devices in a mesh: dp: 16 (over x_lo, y, core), pipe: 16 (over x_hi, z).
Axes of the slice: x: 4 (x_hi: 2, x_lo: 2; x = x_hi * 2 + x_lo), y: 4, z: 8, core: 2. Of those that a mesh axis runs over, the one named last changes fastest.
Arguments:
- hidden: bfloat16 [512, 4608], P(('dp', 'pipe')), may hold values from -6 to 6
- norm_gain: float32 [4608], replicated, may hold values from 0.5 to 1.5
- weight: bfloat16 [131072, 4608], P(('dp', 'pipe')), may hold values from -0.25 to 0.25
- targets: int32 [512], replicated, may hold values from 0 to 131071
Outputs:
- token_loss: float32 [512], P(('dp', 'pipe'))
- grad_hidden: float32 [512, 4608], P(('dp', 'pipe'))
- grad_weight: bfloat16 [131072, 4608], P(('dp', 'pipe'))
- grad_gain: float32 [4608], replicated
All inputs are finite; a program needn't handle non-finite values.
Results may differ from a plain program's by a relative error of at most 0.0055.
Values may be sent and summed in bfloat16 or wider, within the bound.
No kernel may reach another device: no remote copies, remote signals or barrier semaphores. Data moves between devices by JAX's collectives and lax.ppermute only.
A program may use at most 128 MiB of HBM per device.

v0:
```python
import jax
import jax.numpy as jnp
from jax import lax
from jax.sharding import PartitionSpec as P

epsilon = 1e-06
cap_value = 30.0
entropy_weight = 0.2


def on_device(hidden, norm_gain, weight, targets):
    own_rows = hidden.shape[0]
    vocab_rows = weight.shape[0]
    values = hidden.astype(jnp.float32)
    inverse = lax.rsqrt(jnp.mean(values * values, axis=-1, keepdims=True) + epsilon)
    unit_rows = values * inverse
    normed = (unit_rows * norm_gain).astype(jnp.bfloat16)
    gathered = lax.all_gather(normed, ("dp", "pipe"), axis=0, tiled=True)
    logits = lax.dot_general(
        gathered, weight, (((1,), (1,)), ((), ())), preferred_element_type=jnp.float32
    )
    capped = cap_value * jnp.tanh(logits / cap_value)
    powers = jnp.exp(capped - cap_value)
    position = lax.axis_index(("dp", "pipe"))
    columns = position * vocab_rows + lax.iota(jnp.int32, vocab_rows)
    target_hit = targets[:, None] == columns[None, :]
    local_exp = jnp.sum(powers, axis=-1)
    local_weighted = jnp.sum(powers * capped, axis=-1)
    local_target = jnp.sum(jnp.where(target_hit, capped, 0.0), axis=-1)
    total_exp, total_weighted, target_logit = lax.psum(
        (local_exp, local_weighted, local_target), ("dp", "pipe")
    )
    log_total = cap_value + jnp.log(total_exp)
    mean_logit = total_weighted / total_exp
    every_loss = log_total - target_logit - entropy_weight * (log_total - mean_logit)
    token_loss = lax.dynamic_slice_in_dim(every_loss, position * own_rows, own_rows, 0)
    probs = jnp.exp(capped - log_total[:, None])
    raw_grad = (
        probs
        - target_hit.astype(jnp.float32)
        + entropy_weight * probs * (capped - mean_logit[:, None])
    )
    ratio = capped / cap_value
    logit_grad = (raw_grad * (1.0 - ratio * ratio)).astype(jnp.bfloat16)
    grad_weight = lax.dot_general(
        logit_grad, gathered, (((0,), (0,)), ((), ())), preferred_element_type=jnp.float32
    ).astype(jnp.bfloat16)
    grad_normed = lax.psum_scatter(
        jnp.dot(logit_grad, weight, preferred_element_type=jnp.float32),
        ("dp", "pipe"),
        scatter_dimension=0,
        tiled=True,
    )
    grad_gain = lax.psum(jnp.sum(grad_normed * unit_rows, axis=0), ("dp", "pipe"))
    scaled = norm_gain * grad_normed
    grad_hidden = (
        scaled - unit_rows * jnp.mean(scaled * unit_rows, axis=-1, keepdims=True)
    ) * inverse
    return (token_loss, grad_hidden, grad_weight, grad_gain)


def solution(mesh):
    placed = (P(("dp", "pipe"), None), P(), P(("dp", "pipe"), None), P())
    return jax.shard_map(
        on_device,
        mesh=mesh,
        in_specs=placed,
        out_specs=(P(("dp", "pipe")), P(("dp", "pipe"), None), P(("dp", "pipe"), None), P()),
        check_vma=False,
    )
```

profile of v0, /device:TPU:32, one launch (start us, length us, event | category | flops | bytes accessed | tf_op | source)
XLA Modules:
  0.0 1184.0 jit_solution(346657316956187697)
XLA Ops:
  7.2 0.0 all-gather.3.cloned.1.call-start
  7.2 0.9 fusion.18
  8.1 1.4 fusion.19
  9.5 0.0 all-gather.3.cloned.1.call-update
  9.6 0.0 all-reduce.5.cloned.1.call-start
  9.6 0.0 copy-start.2
  9.6 715.1 %all-gather.3.cloned.1.call-done = bf16[256,2,4608]{2,1,0:T(2,128)(2,1)} async-done(((bf16[1,2,4608]{2,1,0:T(2,128)(2,1)}), bf16[256,2,4608]{2,1,0:T(2,128)(2,1)}) %all-gather.3.cloned.1.call-update) | async-done | bytes 4718608 | tf_op jit(solution)/shard_map/all_gather | solution.py:18
  724.7 7.6 reshape.29
  732.3 0.0 copy-done.2
  732.3 6.2 fusion.1
  738.6 75.0 %all-reduce.2 = (f32[512]{0:T(512)S(1)}, f32[512]{0:T(512)S(1)}) all-reduce(f32[512]{0:T(512)S(1)} %get-tuple-element.7, f32[512]{0:T(512)S(1)} %get-tuple-element.8), channel_id=1, replica_groups=mesh['dp'=16,'pipe'=16] {'dp','pipe'}, use_global_device_ids=true, to_apply=%region_6.7 | all-reduce | flops 1024 | bytes 8192 | tf_op jit(solution)/shard_map/psum | solution.py:30
  813.6 7.6 fusion.21
  821.1 0.0 all-reduce.5.cloned.1.call-update
  821.2 0.0 copy-start
  821.2 0.0 copy-start.1
  821.2 7.0 convolution_convert_fusion
  828.2 268.4 %all-reduce.5.cloned.1.call-done = f32[512,4608]{1,0:T(8,128)} async-done(((f32[512,4608]{1,0:T(8,128)}), f32[512,4608]{1,0:T(8,128)}) %all-reduce.5.cloned.1.call-update) | async-done | bytes 9437200
  1096.6 0.0 copy-done
  1096.7 0.0 copy-done.1
  1096.7 1.2 fusion.17
  1097.8 77.1 %all-reduce.1 = (f32[512]{0:T(512)S(1)}, f32[4608]{0:T(1024)}) all-reduce(f32[512]{0:T(512)S(1)} %get-tuple-element.6, f32[4608]{0:T(1024)S(1)} %get-tuple-element.4), channel_id=1, replica_groups=mesh['dp'=16,'pipe'=16] {'dp','pipe'}, use_global_device_ids=true, to_apply=%region_4.5 | all-reduce | flops 5120 | bytes 40960 | tf_op jit(solution)/shard_map/psum | solution.py:30
  1175.0 0.6 dynamic_slice.3
  1175.6 1.6 fusion.16
  (5 shorter events, 0.0 us)
Async XLA Ops:
  7.2 717.6 %all-gather.3.cloned.1.call-start = ((), (), s32[]{:S(2)}) async-start(), calls=%async_computation | async-start | bytes 4737024 | tf_op jit(solution)/shard_map/all_gather | solution.py:18
  9.6 1087.1 %all-reduce.5.cloned.1.call-start = ((), (), s32[]{:S(2)}) async-start(), calls=%async_computation.1 | async-start | bytes 18874368
  9.6 722.7 %copy-start.2 = (s32[512]{0:T(512)S(1)}, s32[512]{0:T(512)}, u32[]{:S(2)}) copy-start(s32[512]{0:T(512)} %param.7) | copy-start | bytes 6148
  821.2 275.5 %copy-start = (bf16[2,4608]{1,0:T(2,128)(2,1)S(1)}, bf16[2,4608]{1,0:T(2,128)(2,1)}, u32[]{:S(2)}) copy-start(bf16[2,4608]{1,0:T(2,128)(2,1)} %param.4) | copy-start | bytes 55300
  821.2 275.5 %copy-start.1 = (f32[4608]{0:T(1024)S(1)}, f32[4608]{0:T(1024)}, u32[]{:S(2)}) copy-start(f32[4608]{0:T(1024)} %param.5) | copy-start | bytes 55300
Sparse Core Ops, SparseCore 0:
  10.5 714.2 all-gather.2
  821.3 275.3 all-reduce.4
where the time goes:
time: 1190 us; the launch traced here: 1180 us
  waiting for transfers between devices  984 us (83%)
  blocking collectives  152 us (13%)
  matrix products  20.8 us (2%)
  between operations  14.1 us (1%)
    all_gather x1, waiting for transfers between devices, on_device(): gathered = lax.all_gather(normed, ('dp', 'pipe'), axis=0, tiled=True)  715 us
    unnamed x3, waiting for transfers between devices  268 us
    psum x2, blocking collectives, on_device(): lax.psum((local_exp, local_weighted, local_target), ('dp', 'pipe'))  152 us
  transfers between devices with their start and end apart: 2, of which 2 were waited for; matrix products, arithmetic and copies ran while one was open for 1% of the time, Pallas kernels for 0%

commit v1 on v0

v1 whole, which is shorter than its diff:
```python
import jax
import jax.numpy as jnp
from jax import lax
from jax.sharding import Mesh, PartitionSpec as P

epsilon = 1e-06
cap_value = 30.0
entropy_weight = 0.2

AXES = ("x_lo", "y", "core", "x_hi", "z")
PLANE = ("x_lo", "y", "x_hi")


def gather_over(block, axes, size):
    copies = jnp.broadcast_to(block[None], (size,) + block.shape)
    return lax.all_to_all(copies, axes, 0, 0, tiled=True)


def sum_over(block, axes, size):
    return jnp.sum(gather_over(block, axes, size), axis=0)


def swap_cores(block):
    return lax.ppermute(block, "core", [(0, 1), (1, 0)])


def on_device(hidden, norm_gain, weight, targets):
    own_rows, width = hidden.shape
    vocab_rows = weight.shape[0]
    values = hidden.astype(jnp.float32)
    inverse = lax.rsqrt(jnp.mean(values * values, axis=-1, keepdims=True) + epsilon)
    unit_rows = values * inverse
    normed = (unit_rows * norm_gain).astype(jnp.bfloat16)

    line = gather_over(normed, "z", 8).reshape(16, width)
    near = gather_over(line, PLANE, 16).reshape(256, width)
    far = swap_cores(near)

    position = lax.axis_index(AXES)
    core = lax.axis_index("core")
    columns = position * vocab_rows + lax.iota(jnp.int32, vocab_rows)
    by_core = targets.reshape(8, 2, 32)
    near_targets = lax.dynamic_index_in_dim(by_core, core, 1, False).reshape(256)
    far_targets = lax.dynamic_index_in_dim(by_core, 1 - core, 1, False).reshape(256)

    def forward(rows, ids):
        logits = lax.dot_general(
            rows, weight, (((1,), (1,)), ((), ())), preferred_element_type=jnp.float32
        )
        capped = cap_value * jnp.tanh(logits / cap_value)
        powers = jnp.exp(capped - cap_value)
        hit = ids[:, None] == columns[None, :]
        sums = jnp.stack([
            jnp.sum(powers, axis=-1),
            jnp.sum(powers * capped, axis=-1),
            jnp.sum(jnp.where(hit, capped, 0.0), axis=-1),
        ])
        return capped, hit, sums

    near_capped, near_hit, near_sums = forward(near, near_targets)
    far_capped, far_hit, far_sums = forward(far, far_targets)
    stats = jnp.stack([near_sums, far_sums], axis=1)
    stats = stats + swap_cores(stats)[:, ::-1]
    stats = sum_over(stats, PLANE, 16)
    stats = sum_over(stats, "z", 8)
    total_exp, total_weighted, target_logit = stats
    log_total = cap_value + jnp.log(total_exp)
    mean_logit = total_weighted / total_exp
    every_loss = log_total - target_logit - entropy_weight * (log_total - mean_logit)
    place = (lax.axis_index(PLANE) * 8 + lax.axis_index("z")) * own_rows
    token_loss = lax.dynamic_slice_in_dim(every_loss[0], place, own_rows, 0)

    def backward(capped, hit, half):
        probs = jnp.exp(capped - log_total[half][:, None])
        raw_grad = (
            probs
            - hit.astype(jnp.float32)
            + entropy_weight * probs * (capped - mean_logit[half][:, None])
        )
        ratio = capped / cap_value
        return (raw_grad * (1.0 - ratio * ratio)).astype(jnp.bfloat16)

    far_grad = backward(far_capped, far_hit, 1)
    far_part = jnp.dot(far_grad, weight, preferred_element_type=jnp.float32).astype(jnp.bfloat16)
    arrived = swap_cores(far_part)
    near_grad = backward(near_capped, near_hit, 0)
    near_part = jnp.dot(near_grad, weight, preferred_element_type=jnp.float32)
    pair_part = (near_part + arrived.astype(jnp.float32)).astype(jnp.bfloat16)
    grad_weight = (
        lax.dot_general(near_grad, near, (((0,), (0,)), ((), ())), preferred_element_type=jnp.float32)
        + lax.dot_general(far_grad, far, (((0,), (0,)), ((), ())), preferred_element_type=jnp.float32)
    ).astype(jnp.bfloat16)
    plane_parts = lax.all_to_all(pair_part.reshape(16, 16, width), PLANE, 0, 0, tiled=True)
    line_part = jnp.sum(plane_parts.astype(jnp.float32), axis=0).astype(jnp.bfloat16)
    line_parts = lax.all_to_all(line_part.reshape(8, 2, width), "z", 0, 0, tiled=True)
    grad_normed = jnp.sum(line_parts.astype(jnp.float32), axis=0)

    gain_part = jnp.sum(grad_normed * unit_rows, axis=0)
    gain_part = sum_over(gain_part, "z", 8)
    gain_part = sum_over(gain_part, PLANE, 16)
    grad_gain = gain_part + swap_cores(gain_part)
    scaled = norm_gain * grad_normed
    grad_hidden = (
        scaled - unit_rows * jnp.mean(scaled * unit_rows, axis=-1, keepdims=True)
    ) * inverse
    return (token_loss, grad_hidden, grad_weight, grad_gain)


def solution(mesh):
    fine = Mesh(mesh.devices.reshape(2, 4, 2, 2, 8), AXES)
    rows = P(AXES, None)
    return jax.shard_map(
        on_device,
        mesh=fine,
        in_specs=(rows, P(), rows, P()),
        out_specs=(P(AXES), rows, rows, P()),
        check_vma=False,
    )
```

time: 1190 us -> 201 us (0.17)
  waiting for transfers between devices: 984 us -> 57.8 us
  blocking collectives: 152 us -> 75.8 us
  starting transfers between devices: 0.08 us -> 22.1 us
  between operations: 14.1 us -> 1.05 us
  matrix products: 20.8 us -> 33.1 us
    all_gather x1 -> x0, waiting for transfers between devices: 715 us -> none  [on_device(): gathered = lax.all_gather(normed, ('dp', 'pipe'), axis=0, tiled=True)]
    unnamed x3 -> x0, waiting for transfers between devices: 268 us -> none
    psum x2 -> x0, blocking collectives: 152 us -> none  [on_device(): lax.psum((local_exp, local_weighted, local_target), ('dp', 'pipe'))]
    all_to_all x0 -> x4, blocking collectives: none -> 75.8 us  [gather_over(): return lax.all_to_all(copies, axes, 0, 0, tiled=True)]
    all_to_all x0 -> x4, waiting for transfers between devices: none -> 47.4 us  [the longest x1 38.5 us: on_device(): lax.all_to_all(pair_part.reshape(16, 16, width), PLANE, 0, 0, tiled=True)]
    all_to_all x0 -> x4, starting transfers between devices: none -> 21.7 us  [the longest x2 13.2 us: gather_over(): return lax.all_to_all(copies, axes, 0, 0, tiled=True)]
    dot_general x3 -> x6, matrix products: 20.8 us -> 33.1 us  [the longest x2 8.57 us: forward(): lax.dot_general(rows, weight, (((1,), (1,)), ((), ())), preferred_element...]
  transfers between devices with their start and end apart: 2 -> 8, of which waited for: 2 -> 7; matrix products, arithmetic and copies ran while one was open for 1% -> 9% of each run, Pallas kernels for 0% -> 0%
where the time goes in v1:
time: 201 us; the launch traced here: 199 us
  blocking collectives  75.8 us (38%)
  waiting for transfers between devices  57.8 us (29%)
  matrix products  33.1 us (16%)
  starting transfers between devices  22.1 us (11%)
  other arithmetic  4.71 us (2%)
  local copies, waits for them, and re-layouts  4.34 us (2%)
    all_to_all x4, blocking collectives, gather_over(): return lax.all_to_all(copies, axes, 0, 0, tiled=True)  75.8 us
    all_to_all x1, waiting for transfers between devices, on_device(): lax.all_to_all(pair_part.reshape(16, 16, width), PLANE, 0, 0, tiled=True)  38.5 us
    all_to_all x2, starting transfers between devices, gather_over(): return lax.all_to_all(copies, axes, 0, 0, tiled=True)  13.2 us
    ppermute x4, waiting for transfers between devices, swap_cores(): return lax.ppermute(block, 'core', [(0, 1), (1, 0)])  10.4 us
    dot_general x2, matrix products, forward(): lax.dot_general(rows, weight, (((1,), (1,)), ((), ())), preferred_element...  8.57 us
    dot_general x1, matrix products, on_device(): lax.dot_general(far_grad, far, (((0,), (0,)), ((), ())), preferred_elemen...  8.28 us
    all_to_all x2, waiting for transfers between devices, gather_over(): return lax.all_to_all(copies, axes, 0, 0, tiled=True)  8.15 us
    dot_general x1, matrix products, on_device(): lax.dot_general(near_grad, near, (((0,), (0,)), ((), ())), preferred_elem...  7.04 us
  transfers between devices with their start and end apart: 8, of which 7 were waited for; matrix products, arithmetic and copies ran while one was open for 9% of the time, Pallas kernels for 0%

profile of v1, /device:TPU:32, one launch (start us, length us, event | category | flops | bytes accessed | tf_op | source)
XLA Modules:
  0.0 199.0 jit_solution(14445295607338572148)
XLA Ops:
  0.6 0.9 fusion.27
  2.0 0.8 fusion.22
  3.0 16.3 %all_to_all.42 = bf16[8,2,4608]{2,1,0:T(2,128)(2,1)S(1)} all-to-all(bf16[8,2,4608]{2,1,0:T(2,128)(2,1)S(1)} %broadcast_in_dim.19), channel_id=1, replica_groups=mesh['x_lo'=2,'y'=4,'core'=2,'x_hi'=2,'z'=8] {'z'}, dimensions={0} | all-to-all | bytes 294912 | tf_op jit(solution)/shard_map/all_to_all | solution.py:16
  19.6 37.0 %all_to_all.43 = bf16[16,16,4608]{2,1,0:T(8,128)(2,1)S(1)} all-to-all(bf16[16,16,4608]{2,1,0:T(8,128)(2,1)S(1)} %broadcast_in_dim.21), channel_id=1, replica_groups=mesh['x_lo'=2,'y'=4,'core'=2,'x_hi'=2,'z'=8] {'x_lo','y','x_hi'}, dimensions={0} | all-to-all | bytes 4718592 | tf_op jit(solution)/shard_map/all_to_all | solution.py:16
  56.8 4.4 %collective-permute-done = bf16[256,4608]{1,0:T(8,128)(2,1)} collective-permute-done((bf16[256,4608]{1,0:T(8,128)(2,1)S(1)}, bf16[256,4608]{1,0:T(8,128)(2,1)}, u32[]{:S(2)}, u32[]{:S(2)}) %collective-permute-start) | collective-permute-done | bytes 2359328 | tf_op jit(solution)/shard_map/ppermute | solution.py:24
  61.2 4.5 %fusion = f32[256,512]{1,0:T(8,128)S(1)} fusion(bf16[256,4608]{1,0:T(8,128)(2,1)} %collective-permute-done, bf16[512,4608]{1,0:T(8,128)(2,1)} %param.6), kind=kOutput, calls=%fused_computation.4 | convolution fusion | flops 1208090624 | bytes 7602176 | tf_op jit(solution)/shard_map/dot_general | solution.py:47
  65.7 4.1 %fusion.16 = (f32[256]{0:T(256)S(1)}, f32[256]{0:T(256)S(1)}, f32[256]{0:T(256)S(1)}, f32[256]{0:T(256)S(1)}, f32[256]{0:T(256)S(1)}, /*index=5*/f32[256]{0:T(256)S(1)}, f32[256,512]{1,0:T(8,128)S(1)}) fusion(s32[512]{0:T(512)S(1)} %iota_add_fusion, s32[256]{0:T(256)S(1)} %eq.28, s32[256]{0:T(256)S(1)} %eq.32, f32[256,512]{1,0:T(8,128)S(1)} %fusion, ...), kind=kOutput, calls=%fused_computation.29 | convolution fusion | flops 1210186240 | bytes 8136704 | tf_op jit(solution)/shard_map/dot_general | solution.py:47
  70.1 1.0 collective-permute-done.1
  71.3 12.7 %all_to_all.44 = f32[16,3,2,256]{3,2,1,0:T(2,128)S(1)} all-to-all(f32[16,3,2,256]{3,2,1,0:T(2,128)S(1)} %broadcast_in_dim.23), channel_id=1, replica_groups=mesh['x_lo'=2,'y'=4,'core'=2,'x_hi'=2,'z'=8] {'x_lo','y','x_hi'}, dimensions={0} | all-to-all | bytes 196608 | tf_op jit(solution)/shard_map/all_to_all | solution.py:16
  84.1 9.8 %all_to_all.45 = f32[8,3,2,256]{3,2,1,0:T(2,128)S(1)} all-to-all(f32[8,3,2,256]{3,2,1,0:T(2,128)S(1)} %broadcast_in_dim.24), channel_id=1, replica_groups=mesh['x_lo'=2,'y'=4,'core'=2,'x_hi'=2,'z'=8] {'z'}, dimensions={0} | all-to-all | bytes 98304 | tf_op jit(solution)/shard_map/all_to_all | solution.py:16
  94.0 3.9 %convolution_convert_fusion = bf16[256,4608]{1,0:T(8,128)(2,1)S(1)} fusion(bf16[512,4608]{1,0:T(8,128)(2,1)} %param.6, f32[256,512]{1,0:T(8,128)S(1)} %fusion, f32[256]{0:T(256)S(1)} %bitcast.32, f32[256]{0:T(256)S(1)} %bitcast.30, s32[512]{0:T(512)S(1)} %iota_add_fusion, s32[256]{0:T(256)S(1)} %eq.32), kind=kOutput, calls=%fused_computation.1 | convolution fusion | flops 1210843136 | bytes 7607296 | tf_op jit(solution)/shard_map/dot_general | solution.py:84
  98.1 4.5 %collective-permute-done.2 = bf16[256,4608]{1,0:T(8,128)(2,1)S(1)} collective-permute-done((bf16[256,4608]{1,0:T(8,128)(2,1)S(1)}, bf16[256,4608]{1,0:T(8,128)(2,1)S(1)}, u32[]{:S(2)}, u32[]{:S(2)}) %collective-permute-start.2) | collective-permute-done | bytes 2359328 | tf_op jit(solution)/shard_map/ppermute | solution.py:24
  102.6 5.3 %add_convert_fusion.1 = bf16[256,4608]{1,0:T(8,128)(2,1)} fusion(bf16[256,4608]{1,0:T(8,128)(2,1)S(1)} %collective-permute-done.2, bf16[512,4608]{1,0:T(8,128)(2,1)} %param.6, f32[256,512]{1,0:T(8,128)S(1)} %get-tuple-element.23, f32[256]{0:T(256)S(1)} %bitcast.28, f32[256]{0:T(256)S(1)} %bitcast.26, s32[512]{0:T(512)S(1)} %iota_add_fusion, s32[256]{0:T(256)S(1)} %eq.28), kind=kOutput, calls=%fused_computation.2 | convolution fusion | flops 1213202432 | bytes 9966592 | tf_op jit(solution)/shard_map/dot_general | solution.py:87
  108.0 3.7 %all-to-all-start.4 = ((bf16[16,16,4608]{2,1,0:T(8,128)(2,1)}), bf16[16,16,4608]{2,1,0:T(8,128)(2,1)S(1)}, u32[]{:S(2)}, u32[]{:S(2)}) async-start(bf16[16,16,4608]{2,1,0:T(8,128)(2,1)} %bitcast.25), calls=%async_computation.4 | async-start | bytes 4718592 | tf_op jit(solution)/shard_map/all_to_all | solution.py:93
  111.7 38.5 %all-to-all-done.4 = bf16[16,16,4608]{2,1,0:T(8,128)(2,1)S(1)} async-done(((bf16[16,16,4608]{2,1,0:T(8,128)(2,1)}), bf16[16,16,4608]{2,1,0:T(8,128)(2,1)S(1)}, u32[]{:S(2)}, u32[]{:S(2)}) %all-to-all-start.4) | async-done | bytes 2359328 | tf_op jit(solution)/shard_map/all_to_all | solution.py:93
  151.2 4.7 %all-to-all-start.5 = ((bf16[8,2,4608]{2,1,0:T(2,128)(2,1)}), bf16[8,2,4608]{2,1,0:T(2,128)(2,1)S(1)}, u32[]{:S(2)}, u32[]{:S(2)}) async-start(bf16[8,2,4608]{2,1,0:T(2,128)(2,1)} %reshape.81), calls=%async_computation.5 | async-start | bytes 294912 | tf_op jit(solution)/shard_map/all_to_all | solution.py:95
  156.0 7.0 %fusion.36 = f32[512,4608]{1,0:T(8,128)} fusion(bf16[256,4608]{1,0:T(8,128)(2,1)} %bitcast.24, f32[256,512]{1,0:T(8,128)S(1)} %get-tuple-element.23, f32[256]{0:T(256)} %bitcast.29, f32[256]{0:T(256)} %bitcast.27, s32[512]{0:T(512)} %copy-done.3, s32[256]{0:T(256)} %copy-done.9), kind=kOutput, calls=%fused_computation.63 | convolution fusion | flops 1209663488 | bytes 12325888 | tf_op jit(solution)/shard_map/dot_general | solution.py:90
  163.1 0.7 all-to-all-done.5
  164.1 0.7 broadcast_in_dim.25
  164.9 6.5 %all-to-all-start.6 = ((f32[8,1,4608]{2,1,0:T(1,128)}), f32[8,1,4608]{2,1,0:T(1,128)S(1)}, u32[]{:S(2)}, u32[]{:S(2)}) async-start(f32[8,1,4608]{2,1,0:T(1,128)} %broadcast_in_dim.25), calls=%async_computation.6 | async-start | bytes 294912 | tf_op jit(solution)/shard_map/all_to_all | solution.py:16
  171.4 8.3 %add_convert_fusion = bf16[512,4608]{1,0:T(8,128)(2,1)} fusion(f32[512,4608]{1,0:T(8,128)} %fusion.36, bf16[256,4608]{1,0:T(8,128)(2,1)} %collective-permute-done, f32[256,512]{1,0:T(8,128)S(1)} %fusion, f32[256]{0:T(256)S(1)} %bitcast.33, f32[256]{0:T(256)S(1)} %bitcast.31, s32[512]{0:T(512)S(1)} %copy-done.4, s32[256]{0:T(256)S(1)} %copy-done.12), kind=kOutput, calls=%fused_computation | convolution fusion | flops 1214382080 | bytes 17044480 | tf_op jit(solution)/shard_map/dot_general | solution.py:91
  180.5 0.9 broadcast_in_dim.26
  181.4 6.7 %all-to-all-start.7 = ((f32[16,1,4608]{2,1,0:T(1,128)}), f32[16,1,4608]{2,1,0:T(1,128)S(1)}, u32[]{:S(2)}, u32[]{:S(2)}) async-start(f32[16,1,4608]{2,1,0:T(1,128)} %broadcast_in_dim.26), calls=%async_computation.7 | async-start | bytes 589824 | tf_op jit(solution)/shard_map/all_to_all | solution.py:16
  188.7 8.1 %all-to-all-done.7 = f32[16,1,4608]{2,1,0:T(1,128)S(1)} async-done(((f32[16,1,4608]{2,1,0:T(1,128)}), f32[16,1,4608]{2,1,0:T(1,128)S(1)}, u32[]{:S(2)}, u32[]{:S(2)}) %all-to-all-start.7) | async-done | bytes 294944 | tf_op jit(solution)/shard_map/all_to_all | solution.py:16
  (79 shorter events, 6.6 us)
Async XLA Ops:
  0.6 55.9 %copy-start.19 = (s32[512]{0:T(512)S(1)}, s32[512]{0:T(512)}, u32[]{:S(2)}) copy-start(s32[512]{0:T(512)} %param.7) | copy-start | bytes 6148
  56.5 13.3 %copy-start = (bf16[16,16,4608]{2,1,0:T(8,128)(2,1)}, bf16[16,16,4608]{2,1,0:T(8,128)(2,1)S(1)}, u32[]{:S(2)}) copy-start(bf16[16,16,4608]{2,1,0:T(8,128)(2,1)S(1)} %all_to_all.43) | copy-start | bytes 7077892
  56.5 4.7 %collective-permute-start = (bf16[256,4608]{1,0:T(8,128)(2,1)S(1)}, bf16[256,4608]{1,0:T(8,128)(2,1)}, u32[]{:S(2)}, u32[]{:S(2)}) collective-permute-start(bf16[256,4608]{1,0:T(8,128)(2,1)S(1)} %bitcast.22), channel_id=1, source_target_pairs={{0,16},{16,0},{1,17},{17,1},{2,18},{18,2},{3,19},{19,3},{4,20},{20... | collective-permute-start | bytes 7077896 | tf_op jit(solution)/shard_map/ppermute | solution.py:24
  56.8 45.8 %copy-start.9 = (s32[256]{0:T(256)}, s32[256]{0:T(256)S(1)}, u32[]{:S(2)}) copy-start(s32[256]{0:T(256)S(1)} %eq.28) | copy-start | bytes 3076
  56.8 37.2 %copy-start.11 = (s32[256]{0:T(256)}, s32[256]{0:T(256)S(1)}, u32[]{:S(2)}) copy-start(s32[256]{0:T(256)S(1)} %eq.32) | copy-start | bytes 3076
  56.8 45.8 %copy-start.3 = (s32[512]{0:T(512)}, s32[512]{0:T(512)S(1)}, u32[]{:S(2)}) copy-start(s32[512]{0:T(512)S(1)} %iota_add_fusion) | copy-start | bytes 6148
  69.9 1.3 collective-permute-start.1
  94.0 8.6 %copy-start.5 = (f32[1,1,256]{2,1,0:T(1,128)}, f32[1,1,256]{2,1,0:T(1,128)S(1)}, u32[]{:S(2)}) copy-start(f32[1,1,256]{2,1,0:T(1,128)S(1)} %get-tuple-element.17) | copy-start | bytes 3076
  94.0 8.6 %copy-start.7 = (f32[1,1,256]{2,1,0:T(1,128)}, f32[1,1,256]{2,1,0:T(1,128)S(1)}, u32[]{:S(2)}) copy-start(f32[1,1,256]{2,1,0:T(1,128)S(1)} %get-tuple-element.24) | copy-start | bytes 3076
  98.0 4.6 %collective-permute-start.2 = (bf16[256,4608]{1,0:T(8,128)(2,1)S(1)}, bf16[256,4608]{1,0:T(8,128)(2,1)S(1)}, u32[]{:S(2)}, u32[]{:S(2)}) collective-permute-start(bf16[256,4608]{1,0:T(8,128)(2,1)S(1)} %convolution_convert_fusion), channel_id=1, source_target_pairs={{0,16},{16,0},{1,17},{17,1},{2,18},{18,2},{3,19},{19,3},{4,20},{20... | collective-permute-start | bytes 7077896 | tf_op jit(solution)/shard_map/ppermute | solution.py:24
  108.0 42.2 %all-to-all-start.4 = ((bf16[16,16,4608]{2,1,0:T(8,128)(2,1)}), bf16[16,16,4608]{2,1,0:T(8,128)(2,1)S(1)}, u32[]{:S(2)}, u32[]{:S(2)}) async-start(bf16[16,16,4608]{2,1,0:T(8,128)(2,1)} %bitcast.25), calls=%async_computation.4 | async-start | bytes 4718592 | tf_op jit(solution)/shard_map/all_to_all | solution.py:93
  151.2 12.6 %all-to-all-start.5 = ((bf16[8,2,4608]{2,1,0:T(2,128)(2,1)}), bf16[8,2,4608]{2,1,0:T(2,128)(2,1)S(1)}, u32[]{:S(2)}, u32[]{:S(2)}) async-start(bf16[8,2,4608]{2,1,0:T(2,128)(2,1)} %reshape.81), calls=%async_computation.5 | async-start | bytes 294912 | tf_op jit(solution)/shard_map/all_to_all | solution.py:95
  156.0 7.9 %copy-start.1 = (bf16[2,4608]{1,0:T(2,128)(2,1)S(1)}, bf16[2,4608]{1,0:T(2,128)(2,1)}, u32[]{:S(2)}) copy-start(bf16[2,4608]{1,0:T(2,128)(2,1)} %param.4) | copy-start | bytes 55300
  156.0 7.9 %copy-start.2 = (f32[4608]{0:T(1024)S(1)}, f32[4608]{0:T(1024)}, u32[]{:S(2)}) copy-start(f32[4608]{0:T(1024)} %param.5) | copy-start | bytes 55300
  156.0 7.9 %copy-start.18 = (f32[2]{0:T(128)S(1)}, f32[2]{0:T(128)}, u32[]{:S(2)}) copy-start(f32[2]{0:T(128)} %copy-done.17) | copy-start | bytes 28
  156.0 15.4 %copy-start.4 = (s32[512]{0:T(512)S(1)}, s32[512]{0:T(512)}, u32[]{:S(2)}) copy-start(s32[512]{0:T(512)} %copy-done.3) | copy-start | bytes 6148
  156.0 15.4 %copy-start.12 = (s32[256]{0:T(256)S(1)}, s32[256]{0:T(256)}, u32[]{:S(2)}) copy-start(s32[256]{0:T(256)} %copy-done.11) | copy-start | bytes 3076
  156.0 15.4 %copy-start.14 = (f32[1,1,256]{2,1,0:T(1,128)S(1)}, f32[1,1,256]{2,1,0:T(1,128)}, u32[]{:S(2)}) copy-start(f32[1,1,256]{2,1,0:T(1,128)} %copy-done.13) | copy-start | bytes 3076
  156.0 15.4 %copy-start.16 = (f32[1,1,256]{2,1,0:T(1,128)S(1)}, f32[1,1,256]{2,1,0:T(1,128)}, u32[]{:S(2)}) copy-start(f32[1,1,256]{2,1,0:T(1,128)} %copy-done.15) | copy-start | bytes 3076
  164.9 15.5 %all-to-all-start.6 = ((f32[8,1,4608]{2,1,0:T(1,128)}), f32[8,1,4608]{2,1,0:T(1,128)S(1)}, u32[]{:S(2)}, u32[]{:S(2)}) async-start(f32[8,1,4608]{2,1,0:T(1,128)} %broadcast_in_dim.25), calls=%async_computation.6 | async-start | bytes 294912 | tf_op jit(solution)/shard_map/all_to_all | solution.py:16
  171.4 16.7 %copy-start.6 = (f32[1,1,256]{2,1,0:T(1,128)S(1)}, f32[1,1,256]{2,1,0:T(1,128)}, u32[]{:S(2)}) copy-start(f32[1,1,256]{2,1,0:T(1,128)} %copy-done.5) | copy-start | bytes 3076
  171.4 16.7 %copy-start.8 = (f32[1,1,256]{2,1,0:T(1,128)S(1)}, f32[1,1,256]{2,1,0:T(1,128)}, u32[]{:S(2)}) copy-start(f32[1,1,256]{2,1,0:T(1,128)} %copy-done.7) | copy-start | bytes 3076
  181.4 15.5 %all-to-all-start.7 = ((f32[16,1,4608]{2,1,0:T(1,128)}), f32[16,1,4608]{2,1,0:T(1,128)S(1)}, u32[]{:S(2)}, u32[]{:S(2)}) async-start(f32[16,1,4608]{2,1,0:T(1,128)} %broadcast_in_dim.26), calls=%async_computation.7 | async-start | bytes 589824 | tf_op jit(solution)/shard_map/all_to_all | solution.py:16
  197.1 1.3 collective-permute-start.3
  (4 other events, 12.5 us)

commit v2 on v0

v2 whole, which is shorter than its diff:
```python
import jax
import jax.numpy as jnp
from jax import lax
from jax.experimental import pallas as pl
from jax.experimental.pallas import tpu as pltpu
from jax.sharding import Mesh, PartitionSpec as P

epsilon = 1e-06
cap_value = 30.0
entropy_weight = 0.2

AXES = ("x_lo", "y", "core", "x_hi", "z")
PLANE = ("x_lo", "y", "x_hi")
WIDTH = 4608
HALF = WIDTH // 2
TOKENS = 512
NEAR = TOKENS // 2
VOCAB_ROWS = 512
PIECE = 16
STEP = 768
STEPS = WIDTH // STEP
HALF_STEPS = HALF // STEP
VMEM_BYTES = 40 * 1024 * 1024

RING = (0, 2, 1, 3)


def shift_y(block, step):
    return lax.ppermute(block, "y", [(p, (p + step) % 4) for p in range(4)])


def shift_x(block, step):
    pairs = [(RING[p], RING[(p + step) % 4]) for p in range(4)]
    return lax.ppermute(block, ("x_lo", "x_hi"), pairs)


def swap_cores(block):
    return lax.ppermute(block, "core", [(0, 1), (1, 0)])


def gather_over(block, axes, size):
    copies = jnp.broadcast_to(block[None], (size,) + block.shape)
    return lax.all_to_all(copies, axes, 0, 0, tiled=True)


def sum_over(block, axes, size):
    return jnp.sum(gather_over(block, axes, size), axis=0)


def gather_ring(block, shift):
    up, down, across = shift(block, 3), shift(block, 1), shift(block, 2)
    return [block, up, across, down]


def scatter_ring(blocks, shift):
    up, down, across = shift(blocks[1], 1), shift(blocks[3], 3), shift(blocks[2], 2)
    return (
        blocks[0].astype(jnp.float32)
        + up.astype(jnp.float32)
        + down.astype(jnp.float32)
        + across.astype(jnp.float32)
    )


def piece_row(core, y, x):
    return pl.multiple_of((core * 16 + y * 4 + x) * PIECE, PIECE)


def forward_kernel(place, targets, weight, *rest):
    blocks = rest[:16]
    gathered, capped_out, stats_out, weight_held, rows_held, weight_sems, row_sems, out_sem = rest[16:]
    core, y, x, position = place[0], place[1], place[2], place[3]

    def half_columns(half):
        return pl.ds(half * HALF, HALF)

    weight_copies = []
    row_copies = ([], [])
    for half in range(2):
        copy = pltpu.make_async_copy(
            weight.at[:, half_columns(half)],
            weight_held.at[:, half_columns(half)],
            weight_sems.at[half],
        )
        copy.start()
        weight_copies.append(copy)
        for far in range(2):
            owner = core if far == 0 else 1 - core
            for outer in range(4):
                block = blocks[far * 8 + half * 4 + outer]
                for inner in range(4):
                    up_y, up_x = (outer, inner) if half == 0 else (inner, outer)
                    row = piece_row(owner, lax.rem(y + up_y, 4), lax.rem(x + up_x, 4))
                    copy = pltpu.make_async_copy(
                        block.at[pl.ds(inner * PIECE, PIECE), :],
                        rows_held.at[pl.ds(row, PIECE), half_columns(half)],
                        row_sems.at[half * 32 + far * 16 + outer * 4 + inner],
                    )
                    copy.start()
                    row_copies[half].append(copy)

    logits = None
    for half in range(2):
        weight_copies[half].wait()
        for copy in row_copies[half]:
            copy.wait()
        columns = slice(half * HALF, (half + 1) * HALF)
        part = lax.dot_general(
            weight_held[:, columns],
            rows_held[:, columns],
            (((1,), (1,)), ((), ())),
            preferred_element_type=jnp.float32,
        )
        logits = part if logits is None else logits + part
    out_copy = pltpu.make_async_copy(rows_held, gathered, out_sem)
    out_copy.start()
    capped = cap_value * jnp.tanh(logits / cap_value)
    capped_out[...] = capped
    powers = jnp.exp(capped - cap_value)
    entry = position * VOCAB_ROWS + lax.broadcasted_iota(jnp.int32, capped.shape, 0)
    hit = targets[...] == entry
    stats_out[0:1, :] = jnp.sum(powers, axis=0, keepdims=True)
    stats_out[1:2, :] = jnp.sum(powers * capped, axis=0, keepdims=True)
    stats_out[2:3, :] = jnp.sum(jnp.where(hit, capped, 0.0), axis=0, keepdims=True)
    out_copy.wait()


def forward(place, targets, weight, blocks):
    vmem, hbm = pl.BlockSpec(memory_space=pltpu.VMEM), pl.BlockSpec(memory_space=pl.ANY)
    return pl.pallas_call(
        forward_kernel,
        out_shape=(
            jax.ShapeDtypeStruct((TOKENS, WIDTH), jnp.bfloat16),
            jax.ShapeDtypeStruct((VOCAB_ROWS, TOKENS), jnp.float32),
            jax.ShapeDtypeStruct((3, TOKENS), jnp.float32),
        ),
        in_specs=[pl.BlockSpec(memory_space=pltpu.SMEM), vmem] + [hbm] * 17,
        out_specs=(hbm, vmem, vmem),
        scratch_shapes=[
            pltpu.VMEM((VOCAB_ROWS, WIDTH), jnp.bfloat16),
            pltpu.VMEM((TOKENS, WIDTH), jnp.bfloat16),
            pltpu.SemaphoreType.DMA((2,)),
            pltpu.SemaphoreType.DMA((64,)),
            pltpu.SemaphoreType.DMA,
        ],
        compiler_params=pltpu.CompilerParams(vmem_limit_bytes=VMEM_BYTES),
        cost_estimate=pl.CostEstimate(
            flops=2 * VOCAB_ROWS * TOKENS * WIDTH, bytes_accessed=16 << 20, transcendentals=1 << 19
        ),
        name="forward",
    )(place, targets, weight, *blocks)


def far_kernel(place, targets, capped, totals, weight, grad_out, turned_out, far_out):
    core, position = place[0], place[3]

    @pl.when(pl.program_id(0) == 0)
    def _():
        log_total = cap_value + jnp.log(totals[0:1, :])
        mean_logit = totals[1:2, :] / totals[0:1, :]
        values = capped[...]
        probs = jnp.exp(values - log_total)
        entry = position * VOCAB_ROWS + lax.broadcasted_iota(jnp.int32, values.shape, 0)
        hit = (targets[...] == entry).astype(jnp.float32)
        raw_grad = probs - hit + entropy_weight * probs * (values - mean_logit)
        ratio = values / cap_value
        grad = raw_grad * (1.0 - ratio * ratio)
        grad_out[...] = grad.astype(jnp.bfloat16)
        turned_out[...] = grad.T.astype(jnp.bfloat16)

    far = pl.multiple_of((1 - core) * NEAR, NEAR)
    far_out[...] = jnp.dot(
        turned_out[pl.ds(far, NEAR), :], weight[...], preferred_element_type=jnp.float32
    ).astype(jnp.bfloat16)


def far_gradient(place, targets, capped, totals, weight):
    whole = lambda rows, columns: pl.BlockSpec((rows, columns), lambda j, place: (0, 0))
    return pl.pallas_call(
        far_kernel,
        out_shape=(
            jax.ShapeDtypeStruct((VOCAB_ROWS, TOKENS), jnp.bfloat16),
            jax.ShapeDtypeStruct((TOKENS, VOCAB_ROWS), jnp.bfloat16),
            jax.ShapeDtypeStruct((NEAR, WIDTH), jnp.bfloat16),
        ),
        grid_spec=pltpu.PrefetchScalarGridSpec(
            num_scalar_prefetch=1,
            grid=(STEPS,),
            in_specs=[
                whole(1, TOKENS),
                whole(VOCAB_ROWS, TOKENS),
                whole(3, TOKENS),
                pl.BlockSpec((VOCAB_ROWS, STEP), lambda j, place: (0, j)),
            ],
            out_specs=[
                whole(VOCAB_ROWS, TOKENS),
                whole(TOKENS, VOCAB_ROWS),
                pl.BlockSpec((NEAR, STEP), lambda j, place: (0, j)),
            ],
        ),
        compiler_params=pltpu.CompilerParams(vmem_limit_bytes=VMEM_BYTES),
        cost_estimate=pl.CostEstimate(
            flops=2 * VOCAB_ROWS * NEAR * WIDTH, bytes_accessed=9 << 20, transcendentals=1 << 18
        ),
        name="far_gradient",
    )(place, targets, capped, totals, weight)


def near_kernel(place, turned, weight, arrived, rows, *rest):
    sends, gain_out, held = rest[:8], rest[8], rest[9]
    y, x = place[1], place[2]
    j = pl.program_id(0)
    part = jnp.dot(turned[...], weight[...], preferred_element_type=jnp.float32)
    part = part + arrived[...].astype(jnp.float32)
    gain_out[...] = jnp.sum(part * rows[...].astype(jnp.float32), axis=0, keepdims=True)
    held[...] = part.reshape(16, PIECE, STEP)

    def store(half):
        for outer in range(4):
            for inner in range(4):
                up_y, up_x = (outer, inner) if half == 0 else (inner, outer)
                piece = held[lax.rem(y + up_y, 4) * 4 + lax.rem(x + up_x, 4)]
                sends[half * 4 + outer][inner * PIECE : (inner + 1) * PIECE, :] = piece.astype(jnp.bfloat16)

    pl.when(j < HALF_STEPS)(lambda: store(0))
    pl.when(j >= HALF_STEPS)(lambda: store(1))


def near_gradient(place, turned, weight, arrived, rows):
    first = pl.BlockSpec((64, STEP), lambda j, place: (0, jnp.minimum(j, HALF_STEPS - 1)))
    second = pl.BlockSpec((64, STEP), lambda j, place: (0, jnp.maximum(j - HALF_STEPS, 0)))
    outs = pl.pallas_call(
        near_kernel,
        out_shape=[jax.ShapeDtypeStruct((64, HALF), jnp.bfloat16)] * 8
        + [jax.ShapeDtypeStruct((1, WIDTH), jnp.float32)],
        grid_spec=pltpu.PrefetchScalarGridSpec(
            num_scalar_prefetch=1,
            grid=(STEPS,),
            in_specs=[
                pl.BlockSpec((NEAR, VOCAB_ROWS), lambda j, place: (place[0], 0)),
                pl.BlockSpec((VOCAB_ROWS, STEP), lambda j, place: (0, j)),
                pl.BlockSpec((NEAR, STEP), lambda j, place: (0, j)),
                pl.BlockSpec((NEAR, STEP), lambda j, place: (place[0], j)),
            ],
            out_specs=[first] * 4 + [second] * 4 + [pl.BlockSpec((1, STEP), lambda j, place: (0, j))],
            scratch_shapes=[pltpu.VMEM((16, PIECE, STEP), jnp.float32)],
        ),
        compiler_params=pltpu.CompilerParams(vmem_limit_bytes=VMEM_BYTES),
        cost_estimate=pl.CostEstimate(
            flops=2 * VOCAB_ROWS * NEAR * WIDTH, bytes_accessed=12 << 20, transcendentals=0
        ),
        name="near_gradient",
    )(place, turned, weight, arrived, rows)
    return outs[:4], outs[4:8], outs[8]


def weight_kernel(grad, rows, out):
    out[...] = jnp.dot(grad[...], rows[...], preferred_element_type=jnp.float32).astype(jnp.bfloat16)


def weight_gradient(grad, rows):
    return pl.pallas_call(
        weight_kernel,
        out_shape=jax.ShapeDtypeStruct((VOCAB_ROWS, WIDTH), jnp.bfloat16),
        grid=(STEPS,),
        in_specs=[
            pl.BlockSpec((VOCAB_ROWS, TOKENS), lambda j: (0, 0)),
            pl.BlockSpec((TOKENS, STEP), lambda j: (0, j)),
        ],
        out_specs=pl.BlockSpec((VOCAB_ROWS, STEP), lambda j: (0, j)),
        compiler_params=pltpu.CompilerParams(vmem_limit_bytes=VMEM_BYTES),
        cost_estimate=pl.CostEstimate(
            flops=2 * VOCAB_ROWS * TOKENS * WIDTH, bytes_accessed=10 << 20, transcendentals=0
        ),
        name="weight_gradient",
    )(grad, rows)


def on_device(hidden, norm_gain, weight, targets):
    core, y, z = lax.axis_index("core"), lax.axis_index("y"), lax.axis_index("z")
    x = lax.axis_index("x_hi") * 2 + lax.axis_index("x_lo")
    place = jnp.stack([core, y, x, lax.axis_index(AXES)]).astype(jnp.int32)
    ids = targets.reshape(2, 4, 2, 2, 16).transpose(2, 1, 3, 0, 4).reshape(1, TOKENS)

    values = hidden.astype(jnp.float32)
    inverse = lax.rsqrt(jnp.mean(values * values, axis=-1, keepdims=True) + epsilon)
    unit_rows = values * inverse
    normed = (unit_rows * norm_gain).astype(jnp.bfloat16)

    line = gather_over(normed, "z", 8).reshape(PIECE, WIDTH)
    first_row = jnp.concatenate(gather_ring(line[:, :HALF], shift_x), axis=0)
    second_row = jnp.concatenate(gather_ring(line[:, HALF:], shift_y), axis=0)
    near_blocks = gather_ring(first_row, shift_y) + gather_ring(second_row, shift_x)
    far_blocks = [swap_cores(block) for block in near_blocks]

    gathered, capped, stats = forward(place, ids, weight, near_blocks + far_blocks)
    stats = stats + swap_cores(stats)
    stats = sum_over(stats, PLANE, 16)
    stats = sum_over(stats, "z", 8)

    grad, turned, far_part = far_gradient(place, ids, capped, stats, weight)
    arrived = swap_cores(far_part)
    first_sends, second_sends, gain_part = near_gradient(place, turned, weight, arrived, gathered)
    first_half = scatter_ring(first_sends, shift_y).astype(jnp.bfloat16)
    second_half = scatter_ring(second_sends, shift_x).astype(jnp.bfloat16)
    grad_weight = weight_gradient(grad, gathered)
    gain_part = sum_over(gain_part, PLANE, 16)

    def pieces(block):
        return [block[k * PIECE : (k + 1) * PIECE] for k in range(4)]

    first_line = scatter_ring(pieces(first_half), shift_x)
    second_line = scatter_ring(pieces(second_half), shift_y)
    line_part = jnp.concatenate([first_line, second_line], axis=1).astype(jnp.bfloat16)
    line_parts = lax.all_to_all(line_part.reshape(8, 2, WIDTH), "z", 0, 0, tiled=True)
    grad_normed = jnp.sum(line_parts.astype(jnp.float32), axis=0)
    gain_part = sum_over(gain_part, "z", 8)
    grad_gain = (gain_part + swap_cores(gain_part)).reshape(WIDTH) / norm_gain

    total_exp, total_weighted, target_logit = stats
    log_total = cap_value + jnp.log(total_exp)
    mean_logit = total_weighted / total_exp
    every_loss = log_total - target_logit - entropy_weight * (log_total - mean_logit)
    row = (core * 16 + y * 4 + x) * PIECE + z * 2
    token_loss = lax.dynamic_slice_in_dim(every_loss, row, 2, 0)
    scaled = norm_gain * grad_normed
    grad_hidden = (
        scaled - unit_rows * jnp.mean(scaled * unit_rows, axis=-1, keepdims=True)
    ) * inverse
    return (token_loss, grad_hidden, grad_weight, grad_gain)


def solution(mesh):
    fine = Mesh(mesh.devices.reshape(2, 4, 2, 2, 8), AXES)
    rows = P(AXES, None)
    return jax.shard_map(
        on_device,
        mesh=fine,
        in_specs=(rows, P(), rows, P()),
        out_specs=(P(AXES), rows, rows, P()),
        check_vma=False,
    )
```

time: 1190 us -> 184 us (0.15)
  waiting for transfers between devices: 984 us -> 31.7 us
  blocking collectives: 152 us -> 41.6 us
  starting transfers between devices: 0.08 us -> 55.1 us
  Pallas kernels: 0 us -> 23.5 us
  matrix products: 20.8 us -> 0 us
  local copies, waits for them, and re-layouts: 8.17 us -> 22.1 us
  between operations: 14.1 us -> 0.93 us
    all_gather x1 -> x0, waiting for transfers between devices: 715 us -> none  [on_device(): gathered = lax.all_gather(normed, ('dp', 'pipe'), axis=0, tiled=True)]
    unnamed x3 -> x0, waiting for transfers between devices: 268 us -> none
    psum x2 -> x0, blocking collectives: 152 us -> none  [on_device(): lax.psum((local_exp, local_weighted, local_target), ('dp', 'pipe'))]
    all_to_all x0 -> x3, blocking collectives: none -> 41.6 us  [gather_over(): return lax.all_to_all(copies, axes, 0, 0, tiled=True)]
    ppermute x0 -> x35, starting transfers between devices: none -> 37.9 us  [the longest x12 18.3 us: shift_x(): return lax.ppermute(block, ('x_lo', 'x_hi'), pairs)]
    ppermute x0 -> x35, waiting for transfers between devices: none -> 26 us  [the longest x12 11.9 us: shift_y(): return lax.ppermute(block, 'y', [(p, (p + step) % 4) for p in range(4)])]
    pallas_call x0 -> x4, Pallas kernels: none -> 23.5 us  [the longest x1 8.2 us: forward(): pl.pallas_call(forward_kernel, out_shape=(jax.ShapeDtypeStruct((TOKENS, W...]
    dot_general x3 -> x0, matrix products: 20.8 us -> none  [the longest x1 7.56 us: on_device(): jnp.dot(logit_grad, weight, preferred_element_type=jnp.float32)]
  transfers between devices with their start and end apart: 2 -> 38, of which waited for: 2 -> 14; matrix products, arithmetic and copies ran while one was open for 1% -> 4% of each run, Pallas kernels for 0% -> 3%
where the time goes in v2:
time: 184 us; the launch traced here: 183 us
  starting transfers between devices  55.1 us (30%)
  blocking collectives  41.6 us (23%)
  waiting for transfers between devices  31.7 us (17%)
  Pallas kernels  23.5 us (13%)
  local copies, waits for them, and re-layouts  22.1 us (12%)
  other arithmetic  7.93 us (4%)
    all_to_all x3, blocking collectives, gather_over(): return lax.all_to_all(copies, axes, 0, 0, tiled=True)  41.6 us
    unnamed x36, local copies, waits for them, and re-layouts  19.3 us
    ppermute x12, starting transfers between devices, shift_x(): return lax.ppermute(block, ('x_lo', 'x_hi'), pairs)  18.3 us
    ppermute x12, starting transfers between devices, shift_y(): return lax.ppermute(block, 'y', [(p, (p + step) % 4) for p in range(4)])  17.8 us
    ppermute x12, waiting for transfers between devices, shift_y(): return lax.ppermute(block, 'y', [(p, (p + step) % 4) for p in range(4)])  11.9 us
    all_to_all x2, starting transfers between devices, gather_over(): return lax.all_to_all(copies, axes, 0, 0, tiled=True)  9.96 us
    pallas_call x1, Pallas kernels, forward(): pl.pallas_call(forward_kernel, out_shape=(jax.ShapeDtypeStruct((TOKENS, W...  8.2 us
    ppermute x12, waiting for transfers between devices, shift_x(): return lax.ppermute(block, ('x_lo', 'x_hi'), pairs)  7.82 us
  transfers between devices with their start and end apart: 38, of which 14 were waited for; matrix products, arithmetic and copies ran while one was open for 4% of the time, Pallas kernels for 3%

profile of v2, /device:TPU:32, one launch (start us, length us, event | category | flops | bytes accessed | tf_op | source)
XLA Modules:
  0.0 182.8 jit_solution(12697447471208142173)
XLA Ops:
  2.4 16.3 %all_to_all.30 = bf16[8,2,4608]{2,1,0:T(2,128)(2,1)S(1)} all-to-all(bf16[8,2,4608]{2,1,0:T(2,128)(2,1)S(1)} %broadcast_in_dim.12), channel_id=1, replica_groups=mesh['x_lo'=2,'y'=4,'core'=2,'x_hi'=2,'z'=8] {'z'}, dimensions={0} | all-to-all | bytes 294912 | tf_op jit(solution)/shard_map/all_to_all | solution.py:43
  20.4 2.7 %collective-permute-start.1 = (bf16[16,2304]{1,0:T(8,128)(2,1)S(1)}, bf16[16,2304]{1,0:T(8,128)(2,1)S(1)}, u32[]{:S(2)}, u32[]{:S(2)}) collective-permute-start(bf16[16,2304]{1,0:T(8,128)(2,1)S(1)} %get-tuple-element.41), channel_id=1, source_target_pairs={{0,8},{128,136},{8,0},{136,128},{1,9},{129,137},{9,1},{137,129},{2... | collective-permute-start | bytes 221192 | tf_op jit(solution)/shard_map/ppermute | solution.py:34
  26.2 2.9 %collective-permute-start.7 = (bf16[16,2304]{1,0:T(8,128)(2,1)S(1)}, bf16[16,2304]{1,0:T(8,128)(2,1)S(1)}, u32[]{:S(2)}, u32[]{:S(2)}) collective-permute-start(bf16[16,2304]{1,0:T(8,128)(2,1)S(1)} %get-tuple-element.40), channel_id=1, source_target_pairs={{0,64},{32,96},{64,0},{96,32},{1,65},{33,97},{65,1},{97,33},{2,66}... | collective-permute-start | bytes 221192 | tf_op jit(solution)/shard_map/ppermute | solution.py:29
  30.6 2.6 %collective-permute-start.4 = (bf16[64,2304]{1,0:T(8,128)(2,1)S(1)}, bf16[64,2304]{1,0:T(8,128)(2,1)S(1)}, u32[]{:S(2)}, u32[]{:S(2)}) collective-permute-start(bf16[64,2304]{1,0:T(8,128)(2,1)S(1)} %pad_maximum_fusion.rest_0_), channel_id=1, source_target_pairs={{0,64},{32,96},{64,0},{96,32},{1,65},{33,97},{65,1},{97,33},{2,66}... | collective-permute-start | bytes 884744 | tf_op jit(solution)/shard_map/ppermute | solution.py:29
  37.0 3.6 %collective-permute-done.3.rest_1_ = bf16[64,2304]{1,0:T(8,128)(2,1)S(1)} collective-permute-done((bf16[64,2304]{1,0:T(8,128)(2,1)S(1)}, bf16[64,2304]{1,0:T(8,128)(2,1)S(1)}, u32[]{:S(2)}, u32[]{:S(2)}) %collective-permute-start.3) | collective-permute-done | bytes 294944 | tf_op jit(solution)/shard_map/ppermute | solution.py:29
  41.7 3.1 %collective-permute-done.5.rest_3_ = bf16[64,2304]{1,0:T(8,128)(2,1)S(1)} collective-permute-done((bf16[64,2304]{1,0:T(8,128)(2,1)S(1)}, bf16[64,2304]{1,0:T(8,128)(2,1)S(1)}, u32[]{:S(2)}, u32[]{:S(2)}) %collective-permute-start.5) | collective-permute-done | bytes 294944 | tf_op jit(solution)/shard_map/ppermute | solution.py:29
  45.4 3.2 %collective-permute-done.11.rest_7_ = bf16[64,2304]{1,0:T(8,128)(2,1)S(1)} collective-permute-done((bf16[64,2304]{1,0:T(8,128)(2,1)S(1)}, bf16[64,2304]{1,0:T(8,128)(2,1)S(1)}, u32[]{:S(2)}, u32[]{:S(2)}) %collective-permute-start.11) | collective-permute-done | bytes 294944 | tf_op jit(solution)/shard_map/ppermute | solution.py:34
  60.7 8.2 %forward.1 = (bf16[512,4608]{1,0:T(8,128)(2,1)S(1)}, f32[512,512]{1,0:T(8,128)S(1)}, f32[3,512]{1,0:T(4,128)S(1)}) custom-call(s32[4]{0:T(128)S(1)} %pad_add_fusion.place, s32[1,512]{1,0:T(1,128)S(1)} %reshape.59.targets, bf16[512,4608]{1,0:T(8,128)(2,1)} %weight.5, bf16[64,2304]{1,0:T(8,128)(2,1)S(1)} %pad_maximum_fusion.rest_0_, ...), custom_call_target="tpu_custom_call" | custom-call | flops 2415919104 | bytes 16777216 | tf_op jit(solution)/shard_map/forward/pallas_call | solution.py:130
  72.3 14.6 %all_to_all.31 = f32[16,3,512]{2,1,0:T(4,128)S(1)} all-to-all(f32[16,3,512]{2,1,0:T(4,128)S(1)} %broadcast_in_dim.13), channel_id=1, replica_groups=mesh['x_lo'=2,'y'=4,'core'=2,'x_hi'=2,'z'=8] {'x_lo','y','x_hi'}, dimensions={0} | all-to-all | bytes 196608 | tf_op jit(solution)/shard_map/all_to_all | solution.py:43
  87.0 10.7 %all_to_all.32 = f32[8,3,512]{2,1,0:T(4,128)S(1)} all-to-all(f32[8,3,512]{2,1,0:T(4,128)S(1)} %broadcast_in_dim.14), channel_id=1, replica_groups=mesh['x_lo'=2,'y'=4,'core'=2,'x_hi'=2,'z'=8] {'z'}, dimensions={0} | all-to-all | bytes 98304 | tf_op jit(solution)/shard_map/all_to_all | solution.py:43
  97.7 2.3 %copy-done = bf16[512,4608]{1,0:T(8,128)(2,1)S(1)} copy-done((bf16[512,4608]{1,0:T(8,128)(2,1)S(1)}, bf16[512,4608]{1,0:T(8,128)(2,1)}, u32[]{:S(2)}) %copy-start) | copy-done | bytes 4718616
  100.0 3.9 %far_gradient.1 = (bf16[512,512]{1,0:T(8,128)(2,1)S(1)}, bf16[512,512]{1,0:T(8,128)(2,1)S(1)}, bf16[256,4608]{1,0:T(8,128)(2,1)S(1)}) custom-call(s32[4]{0:T(128)S(1)} %pad_add_fusion.place, s32[1,512]{1,0:T(1,128)S(1)} %reshape.59.targets, f32[512,512]{1,0:T(8,128)S(1)} %get-tuple-element.20.capped, f32[3,512]{1,0:T(4,128)S(1)} %reduce_sum.67.totals, ...), custom_call_target="tpu_custom_call" | custom-call | flops 1207959552 | bytes 9437184 | tf_op jit(solution)/shard_map/far_gradient/pallas_call | solution.py:179
  104.1 4.5 %collective-permute-done.21.arrived = bf16[256,4608]{1,0:T(8,128)(2,1)S(1)} collective-permute-done((bf16[256,4608]{1,0:T(8,128)(2,1)S(1)}, bf16[256,4608]{1,0:T(8,128)(2,1)S(1)}, u32[]{:S(2)}, u32[]{:S(2)}) %collective-permute-start.21) | collective-permute-done | bytes 2359328 | tf_op jit(solution)/shard_map/ppermute | solution.py:38
  108.6 2.3 %copy-done.1 = bf16[512,4608]{1,0:T(8,128)(2,1)S(1)} copy-done((bf16[512,4608]{1,0:T(8,128)(2,1)S(1)}, bf16[512,4608]{1,0:T(8,128)(2,1)}, u32[]{:S(2)}) %copy-start.1) | copy-done | bytes 4718616
  110.9 6.2 %near_gradient.1 = (bf16[64,2304]{1,0:T(8,128)(2,1)S(1)}, bf16[64,2304]{1,0:T(8,128)(2,1)S(1)}, bf16[64,2304]{1,0:T(8,128)(2,1)S(1)}, bf16[64,2304]{1,0:T(8,128)...) custom-call(s32[4]{0:T(128)S(1)} %pad_add_fusion.place, ...), custom_call_target="tpu_custom_call" | custom-call | flops 1207959552 | bytes 12582912 | tf_op jit(solution)/shard_map/near_gradient/pallas_call | solution.py:232
  121.4 5.2 %all-to-all-start.4 = ((f32[16,1,4608]{2,1,0:T(1,128)}), f32[16,1,4608]{2,1,0:T(1,128)S(1)}, u32[]{:S(2)}, u32[]{:S(2)}) async-start(f32[16,1,4608]{2,1,0:T(1,128)} %broadcast_in_dim.16), calls=%async_computation.4 | async-start | bytes 589824 | tf_op jit(solution)/shard_map/all_to_all | solution.py:43
  126.6 2.3 %copy-done.3 = bf16[512,4608]{1,0:T(8,128)(2,1)S(1)} copy-done((bf16[512,4608]{1,0:T(8,128)(2,1)S(1)}, bf16[512,4608]{1,0:T(8,128)(2,1)}, u32[]{:S(2)}) %copy-start.3) | copy-done | bytes 4718616
  129.0 5.2 %weight_gradient.1 = bf16[512,4608]{1,0:T(8,128)(2,1)} custom-call(bf16[512,512]{1,0:T(8,128)(2,1)S(1)} %get-tuple-element.32.grad, bf16[512,4608]{1,0:T(8,128)(2,1)S(1)} %copy-done.3), custom_call_target="tpu_custom_call" | custom-call | flops 2415919104 | bytes 10485760 | tf_op jit(solution)/shard_map/weight_gradient/pallas_call | solution.py:262
  134.2 3.4 %collective-permute-start.24 = (bf16[64,2304]{1,0:T(8,128)(2,1)S(1)}, bf16[64,2304]{1,0:T(8,128)(2,1)}, u32[]{:S(2)}, u32[]{:S(2)}) collective-permute-start(bf16[64,2304]{1,0:T(8,128)(2,1)S(1)} %get-tuple-element.27), channel_id=1, source_target_pairs={{0,64},{32,96},{64,0},{96,32},{1,65},{33,97},{65,1},{97,33},{2,66}... | collective-permute-start | bytes 884744 | tf_op jit(solution)/shard_map/ppermute | solution.py:29
  139.7 4.7 %all-to-all-start.5 = ((f32[8,1,4608]{2,1,0:T(1,128)}), f32[8,1,4608]{2,1,0:T(1,128)S(1)}, u32[]{:S(2)}, u32[]{:S(2)}) async-start(f32[8,1,4608]{2,1,0:T(1,128)} %broadcast_in_dim.17), calls=%async_computation.5 | async-start | bytes 294912 | tf_op jit(solution)/shard_map/all_to_all | solution.py:43
  155.3 3.8 %collective-permute-start.27 = (bf16[16,2304]{1,0:T(8,128)(2,1)S(1)}, bf16[16,2304]{1,0:T(8,128)(2,1)S(1)}, u32[]{:S(2)}, u32[]{:S(2)}) collective-permute-start(bf16[16,2304]{1,0:T(8,128)(2,1)S(1)} %get-tuple-element.35), channel_id=1, source_target_pairs={{0,8},{128,136},{8,0},{136,128},{1,9},{129,137},{9,1},{137,129},{2... | collective-permute-start | bytes 221192 | tf_op jit(solution)/shard_map/ppermute | solution.py:34
  163.4 2.4 %collective-permute-done.25 = bf16[16,2304]{1,0:T(8,128)(2,1)S(1)} collective-permute-done((bf16[16,2304]{1,0:T(8,128)(2,1)S(1)}, bf16[16,2304]{1,0:T(8,128)(2,1)S(1)}, u32[]{:S(2)}, u32[]{:S(2)}) %collective-permute-start.25) | collective-permute-done | bytes 73760 | tf_op jit(solution)/shard_map/ppermute | solution.py:34
  166.7 7.2 %all-to-all-start.3 = ((bf16[8,2,4608]{2,1,0:T(2,128)(2,1)}), bf16[8,2,4608]{2,1,0:T(2,128)(2,1)S(1)}, u32[]{:S(2)}, u32[]{:S(2)}) async-start(bf16[8,2,4608]{2,1,0:T(2,128)(2,1)} %pad_maximum_fusion.2), calls=%async_computation.3 | async-start | bytes 294912 | tf_op jit(solution)/shard_map/all_to_all | solution.py:315
  176.0 5.7 %all-to-all-done.3 = bf16[8,2,4608]{2,1,0:T(2,128)(2,1)S(1)} async-done(((bf16[8,2,4608]{2,1,0:T(2,128)(2,1)}), bf16[8,2,4608]{2,1,0:T(2,128)(2,1)S(1)}, u32[]{:S(2)}, u32[]{:S(2)}) %all-to-all-start.3) | async-done | bytes 147488 | tf_op jit(solution)/shard_map/all_to_all | solution.py:315
  (135 shorter events, 54.7 us)
Async XLA Ops:
  18.9 10.2 %collective-permute-start.2 = (bf16[16,2304]{1,0:T(8,128)(2,1)S(1)}, bf16[16,2304]{1,0:T(8,128)(2,1)S(1)}, u32[]{:S(2)}, u32[]{:S(2)}) collective-permute-start(bf16[16,2304]{1,0:T(8,128)(2,1)S(1)} %get-tuple-element.41), channel_id=1, source_target_pairs={{0,128},{128,8},{8,136},{136,0},{1,129},{129,9},{9,137},{137,1},{2... | collective-permute-start | bytes 221192 | tf_op jit(solution)/shard_map/ppermute | solution.py:34
  20.4 10.0 %collective-permute-start.1 = (bf16[16,2304]{1,0:T(8,128)(2,1)S(1)}, bf16[16,2304]{1,0:T(8,128)(2,1)S(1)}, u32[]{:S(2)}, u32[]{:S(2)}) collective-permute-start(bf16[16,2304]{1,0:T(8,128)(2,1)S(1)} %get-tuple-element.41), channel_id=1, source_target_pairs={{0,8},{128,136},{8,0},{136,128},{1,9},{129,137},{9,1},{137,129},{2... | collective-permute-start | bytes 221192 | tf_op jit(solution)/shard_map/ppermute | solution.py:34
  23.2 7.3 %collective-permute-start = (bf16[16,2304]{1,0:T(8,128)(2,1)S(1)}, bf16[16,2304]{1,0:T(8,128)(2,1)S(1)}, u32[]{:S(2)}, u32[]{:S(2)}) collective-permute-start(bf16[16,2304]{1,0:T(8,128)(2,1)S(1)} %get-tuple-element.41), channel_id=1, source_target_pairs={{0,136},{128,0},{8,128},{136,8},{1,137},{129,1},{9,129},{137,9},{2... | collective-permute-start | bytes 221192 | tf_op jit(solution)/shard_map/ppermute | solution.py:34
  24.6 8.7 %collective-permute-start.8 = (bf16[16,2304]{1,0:T(8,128)(2,1)S(1)}, bf16[16,2304]{1,0:T(8,128)(2,1)S(1)}, u32[]{:S(2)}, u32[]{:S(2)}) collective-permute-start(bf16[16,2304]{1,0:T(8,128)(2,1)S(1)} %get-tuple-element.40), channel_id=1, source_target_pairs={{0,32},{32,64},{64,96},{96,0},{1,33},{33,65},{65,97},{97,1},{2,34}... | collective-permute-start | bytes 221192 | tf_op jit(solution)/shard_map/ppermute | solution.py:29
  26.2 7.1 %collective-permute-start.7 = (bf16[16,2304]{1,0:T(8,128)(2,1)S(1)}, bf16[16,2304]{1,0:T(8,128)(2,1)S(1)}, u32[]{:S(2)}, u32[]{:S(2)}) collective-permute-start(bf16[16,2304]{1,0:T(8,128)(2,1)S(1)} %get-tuple-element.40), channel_id=1, source_target_pairs={{0,64},{32,96},{64,0},{96,32},{1,65},{33,97},{65,1},{97,33},{2,66}... | collective-permute-start | bytes 221192 | tf_op jit(solution)/shard_map/ppermute | solution.py:29
  30.4 10.1 %collective-permute-start.3 = (bf16[64,2304]{1,0:T(8,128)(2,1)S(1)}, bf16[64,2304]{1,0:T(8,128)(2,1)S(1)}, u32[]{:S(2)}, u32[]{:S(2)}) collective-permute-start(bf16[64,2304]{1,0:T(8,128)(2,1)S(1)} %pad_maximum_fusion.rest_0_), channel_id=1, source_target_pairs={{0,96},{32,0},{64,32},{96,64},{1,97},{33,1},{65,33},{97,65},{2,98}... | collective-permute-start | bytes 884744 | tf_op jit(solution)/shard_map/ppermute | solution.py:29
  30.6 11.1 %collective-permute-start.4 = (bf16[64,2304]{1,0:T(8,128)(2,1)S(1)}, bf16[64,2304]{1,0:T(8,128)(2,1)S(1)}, u32[]{:S(2)}, u32[]{:S(2)}) collective-permute-start(bf16[64,2304]{1,0:T(8,128)(2,1)S(1)} %pad_maximum_fusion.rest_0_), channel_id=1, source_target_pairs={{0,64},{32,96},{64,0},{96,32},{1,65},{33,97},{65,1},{97,33},{2,66}... | collective-permute-start | bytes 884744 | tf_op jit(solution)/shard_map/ppermute | solution.py:29
  33.3 11.5 %collective-permute-start.5 = (bf16[64,2304]{1,0:T(8,128)(2,1)S(1)}, bf16[64,2304]{1,0:T(8,128)(2,1)S(1)}, u32[]{:S(2)}, u32[]{:S(2)}) collective-permute-start(bf16[64,2304]{1,0:T(8,128)(2,1)S(1)} %pad_maximum_fusion.rest_0_), channel_id=1, source_target_pairs={{0,32},{32,64},{64,96},{96,0},{1,33},{33,65},{65,97},{97,1},{2,34}... | collective-permute-start | bytes 884744 | tf_op jit(solution)/shard_map/ppermute | solution.py:29
  34.3 10.5 %collective-permute-start.9 = (bf16[64,2304]{1,0:T(8,128)(2,1)S(1)}, bf16[64,2304]{1,0:T(8,128)(2,1)S(1)}, u32[]{:S(2)}, u32[]{:S(2)}) collective-permute-start(bf16[64,2304]{1,0:T(8,128)(2,1)S(1)} %pad_maximum_fusion.1.rest_4_), channel_id=1, source_target_pairs={{0,136},{128,0},{8,128},{136,8},{1,137},{129,1},{9,129},{137,9},{2... | collective-permute-start | bytes 884744 | tf_op jit(solution)/shard_map/ppermute | solution.py:34
  35.0 10.4 %collective-permute-start.10 = (bf16[64,2304]{1,0:T(8,128)(2,1)S(1)}, bf16[64,2304]{1,0:T(8,128)(2,1)S(1)}, u32[]{:S(2)}, u32[]{:S(2)}) collective-permute-start(bf16[64,2304]{1,0:T(8,128)(2,1)S(1)} %pad_maximum_fusion.1.rest_4_), channel_id=1, source_target_pairs={{0,8},{128,136},{8,0},{136,128},{1,9},{129,137},{9,1},{137,129},{2... | collective-permute-start | bytes 884744 | tf_op jit(solution)/shard_map/ppermute | solution.py:34
  40.6 8.0 %collective-permute-start.11 = (bf16[64,2304]{1,0:T(8,128)(2,1)S(1)}, bf16[64,2304]{1,0:T(8,128)(2,1)S(1)}, u32[]{:S(2)}, u32[]{:S(2)}) collective-permute-start(bf16[64,2304]{1,0:T(8,128)(2,1)S(1)} %pad_maximum_fusion.1.rest_4_), channel_id=1, source_target_pairs={{0,128},{128,8},{8,136},{136,0},{1,129},{129,9},{9,137},{137,1},{2... | collective-permute-start | bytes 884744 | tf_op jit(solution)/shard_map/ppermute | solution.py:34
  45.3 7.4 %collective-permute-start.14 = (bf16[64,2304]{1,0:T(8,128)(2,1)S(1)}, bf16[64,2304]{1,0:T(8,128)(2,1)}, u32[]{:S(2)}, u32[]{:S(2)}) collective-permute-start(bf16[64,2304]{1,0:T(8,128)(2,1)S(1)} %collective-permute-done.4.rest_2_), channel_id=1, source_target_pairs={{0,16},{16,0},{1,17},{17,1},{2,18},{18,2},{3,19},{19,3},{4,20},{20... | collective-permute-start | bytes 884744 | tf_op jit(solution)/shard_map/ppermute | solution.py:38
  117.1 27.3 %collective-permute-start.30 = (bf16[64,2304]{1,0:T(8,128)(2,1)S(1)}, bf16[64,2304]{1,0:T(8,128)(2,1)}, u32[]{:S(2)}, u32[]{:S(2)}) collective-permute-start(bf16[64,2304]{1,0:T(8,128)(2,1)S(1)} %get-tuple-element.31), channel_id=1, source_target_pairs={{0,8},{128,136},{8,0},{136,128},{1,9},{129,137},{9,1},{137,129},{2... | collective-permute-start | bytes 884744 | tf_op jit(solution)/shard_map/ppermute | solution.py:34
  118.2 27.1 %collective-permute-start.29 = (bf16[64,2304]{1,0:T(8,128)(2,1)S(1)}, bf16[64,2304]{1,0:T(8,128)(2,1)}, u32[]{:S(2)}, u32[]{:S(2)}) collective-permute-start(bf16[64,2304]{1,0:T(8,128)(2,1)S(1)} %get-tuple-element.30), channel_id=1, source_target_pairs={{0,136},{128,0},{8,128},{136,8},{1,137},{129,1},{9,129},{137,9},{2... | collective-permute-start | bytes 884744 | tf_op jit(solution)/shard_map/ppermute | solution.py:34
  120.4 24.9 %collective-permute-start.28 = (bf16[64,2304]{1,0:T(8,128)(2,1)S(1)}, bf16[64,2304]{1,0:T(8,128)(2,1)}, u32[]{:S(2)}, u32[]{:S(2)}) collective-permute-start(bf16[64,2304]{1,0:T(8,128)(2,1)S(1)} %get-tuple-element.29), channel_id=1, source_target_pairs={{0,128},{128,8},{8,136},{136,0},{1,129},{129,9},{9,137},{137,1},{2... | collective-permute-start | bytes 884744 | tf_op jit(solution)/shard_map/ppermute | solution.py:34
  121.4 17.4 %all-to-all-start.4 = ((f32[16,1,4608]{2,1,0:T(1,128)}), f32[16,1,4608]{2,1,0:T(1,128)S(1)}, u32[]{:S(2)}, u32[]{:S(2)}) async-start(f32[16,1,4608]{2,1,0:T(1,128)} %broadcast_in_dim.16), calls=%async_computation.4 | async-start | bytes 589824 | tf_op jit(solution)/shard_map/all_to_all | solution.py:43
  134.2 15.8 %collective-permute-start.24 = (bf16[64,2304]{1,0:T(8,128)(2,1)S(1)}, bf16[64,2304]{1,0:T(8,128)(2,1)}, u32[]{:S(2)}, u32[]{:S(2)}) collective-permute-start(bf16[64,2304]{1,0:T(8,128)(2,1)S(1)} %get-tuple-element.27), channel_id=1, source_target_pairs={{0,64},{32,96},{64,0},{96,32},{1,65},{33,97},{65,1},{97,33},{2,66}... | collective-permute-start | bytes 884744 | tf_op jit(solution)/shard_map/ppermute | solution.py:29
  137.6 14.2 %collective-permute-start.23 = (bf16[64,2304]{1,0:T(8,128)(2,1)S(1)}, bf16[64,2304]{1,0:T(8,128)(2,1)}, u32[]{:S(2)}, u32[]{:S(2)}) collective-permute-start(bf16[64,2304]{1,0:T(8,128)(2,1)S(1)} %get-tuple-element.26), channel_id=1, source_target_pairs={{0,96},{32,0},{64,32},{96,64},{1,97},{33,1},{65,33},{97,65},{2,98}... | collective-permute-start | bytes 884744 | tf_op jit(solution)/shard_map/ppermute | solution.py:29
  139.7 27.0 %all-to-all-start.5 = ((f32[8,1,4608]{2,1,0:T(1,128)}), f32[8,1,4608]{2,1,0:T(1,128)S(1)}, u32[]{:S(2)}, u32[]{:S(2)}) async-start(f32[8,1,4608]{2,1,0:T(1,128)} %broadcast_in_dim.17), calls=%async_computation.5 | async-start | bytes 294912 | tf_op jit(solution)/shard_map/all_to_all | solution.py:43
  144.4 9.6 %collective-permute-start.22 = (bf16[64,2304]{1,0:T(8,128)(2,1)S(1)}, bf16[64,2304]{1,0:T(8,128)(2,1)S(1)}, u32[]{:S(2)}, u32[]{:S(2)}) collective-permute-start(bf16[64,2304]{1,0:T(8,128)(2,1)S(1)} %get-tuple-element.25), channel_id=1, source_target_pairs={{0,32},{32,64},{64,96},{96,0},{1,33},{33,65},{65,97},{97,1},{2,34}... | collective-permute-start | bytes 884744 | tf_op jit(solution)/shard_map/ppermute | solution.py:29
  146.6 13.7 %collective-permute-start.33 = (bf16[16,2304]{1,0:T(8,128)(2,1)S(1)}, bf16[16,2304]{1,0:T(8,128)(2,1)S(1)}, u32[]{:S(2)}, u32[]{:S(2)}) collective-permute-start(bf16[16,2304]{1,0:T(8,128)(2,1)S(1)} %get-tuple-element.38), channel_id=1, source_target_pairs={{0,64},{32,96},{64,0},{96,32},{1,65},{33,97},{65,1},{97,33},{2,66}... | collective-permute-start | bytes 221192 | tf_op jit(solution)/shard_map/ppermute | solution.py:29
  148.3 12.8 %collective-permute-start.32 = (bf16[16,2304]{1,0:T(8,128)(2,1)S(1)}, bf16[16,2304]{1,0:T(8,128)(2,1)S(1)}, u32[]{:S(2)}, u32[]{:S(2)}) collective-permute-start(bf16[16,2304]{1,0:T(8,128)(2,1)S(1)} %get-tuple-element.39), channel_id=1, source_target_pairs={{0,96},{32,0},{64,32},{96,64},{1,97},{33,1},{65,33},{97,65},{2,98}... | collective-permute-start | bytes 221192 | tf_op jit(solution)/shard_map/ppermute | solution.py:29
  149.9 11.2 %collective-permute-start.31 = (bf16[16,2304]{1,0:T(8,128)(2,1)S(1)}, bf16[16,2304]{1,0:T(8,128)(2,1)S(1)}, u32[]{:S(2)}, u32[]{:S(2)}) collective-permute-start(bf16[16,2304]{1,0:T(8,128)(2,1)S(1)} %get-tuple-element.37), channel_id=1, source_target_pairs={{0,32},{32,64},{64,96},{96,0},{1,33},{33,65},{65,97},{97,1},{2,34}... | collective-permute-start | bytes 221192 | tf_op jit(solution)/shard_map/ppermute | solution.py:29
  166.7 15.0 %all-to-all-start.3 = ((bf16[8,2,4608]{2,1,0:T(2,128)(2,1)}), bf16[8,2,4608]{2,1,0:T(2,128)(2,1)S(1)}, u32[]{:S(2)}, u32[]{:S(2)}) async-start(bf16[8,2,4608]{2,1,0:T(2,128)(2,1)} %pad_maximum_fusion.2), calls=%async_computation.3 | async-start | bytes 294912 | tf_op jit(solution)/shard_map/all_to_all | solution.py:315
  (32 other events, 167.8 us)
